TPU v7x, 128 devices: a whole 4x4x4 slice. The times are simulated.
128 devices in a mesh: ep: 16 (over x, z), tp: 8 (over y, core).
Axes of the slice: x: 4, y: 4, z: 4, core: 2. Of those that a mesh axis runs over, the one named last changes fastest.
Arguments:
- tokens: bfloat16 [2048, 4096], P('ep', 'tp'), may hold values from -6 to 6
- out_grad: bfloat16 [2048, 4096], P('ep', 'tp'), may hold values from -6 to 6
- routes: int32 [2048, 4], P('ep'), may hold values from 0 to 15, all different within a row; in each aligned block of 128 rows (0 to 127, 128 to 255, ...) at most 64 rows name the same one
- probs: bfloat16 [2048, 4], P('ep'), may hold values from 0.019897461 to 0.59765625
- w_in: bfloat16 [16, 2, 1536, 4096], P('ep', None, 'tp'), as said below
- w_out: bfloat16 [16, 1536, 4096], P('ep', 'tp'), as said below
Outputs:
- in_grad: bfloat16 [2048, 4096], P('ep', 'tp')
- grad_in: bfloat16 [16, 2, 1536, 4096], P('ep', None, 'tp')
- grad_out: bfloat16 [16, 1536, 4096], P('ep', 'tp')
Inputs may be any that keep to these rules, and one draw needn't show every extreme that they name: `routes`: each token names 4 different copies; within the tokens of one device (aligned blocks of 128 tokens) no copy is named more than 64 times, a bound that some block reaches. `w_in`: copies c and c + 8 hold equal weights. `w_out`: copies c and c + 8 hold equal weights.
All inputs are finite; a program needn't handle non-finite values.
Results may differ from a plain program's by a relative error of at most 0.02.
Values may be sent and summed in bfloat16 or wider, within the bound.
A program may use at most 128 MiB of HBM per device.

v0:
```python
import jax
import jax.numpy as jnp
from jax import lax
from jax.sharding import PartitionSpec as P


def partner(block, axis, apart):
    count = lax.axis_size(axis)
    route = []
    for low in range(count):
        high = low | 1 << apart
        if high != low and high < count:
            route += [(low, high), (high, low)]
    return lax.ppermute(block, axis, route)


def slot_tables(block_routes, copies, cap):
    flat = block_routes.reshape(-1)
    nrows = flat.shape[0]
    onehot = (flat[:, None] == jnp.arange(copies, dtype=jnp.int32)[None, :]).astype(jnp.int32)
    ranks = jnp.sum((jnp.cumsum(onehot, axis=0) - 1) * onehot, axis=1)
    slot = flat * cap + ranks
    source = (
        jnp.full((copies * cap,), nrows, jnp.int32).at[slot].set(jnp.arange(nrows, dtype=jnp.int32))
    )
    return (slot, source)


def body(tokens, out_grad, routes, probs, w_in, w_out):
    n_ep = lax.axis_size("ep")
    tok_dev, top = routes.shape
    nrows = tok_dev * top
    cap = 2 * nrows // n_ep
    slot, source = slot_tables(routes, n_ep, cap)
    valid = source < nrows
    local = jnp.minimum(source, nrows - 1)
    tok_index = local // top
    scale = jnp.where(valid, probs.reshape(-1)[local].astype(jnp.float32), 0.0)[:, None]
    full_x, full_g = (
        lax.all_gather(tokens, "tp", axis=1, tiled=True),
        lax.all_gather(out_grad, "tp", axis=1, tiled=True),
    )
    packed_x = jnp.where(valid[:, None], full_x[tok_index], jnp.zeros((), jnp.bfloat16))
    packed_g = (scale * full_g[tok_index].astype(jnp.float32)).astype(jnp.bfloat16)
    width = full_x.shape[1]
    send_x = packed_x.reshape(n_ep, cap, width)
    send_g = packed_g.reshape(n_ep, cap, width)
    recv_x, recv_g = (
        lax.all_to_all(send_x, "ep", split_axis=0, concat_axis=0, tiled=True),
        lax.all_to_all(send_g, "ep", split_axis=0, concat_axis=0, tiled=True),
    )
    width = recv_x.shape[2]
    rows_x = recv_x.reshape(n_ep * cap, width)
    rows_g = recv_g.reshape(n_ep * cap, width)
    w_gate = w_in[0, 0]
    w_up = w_in[0, 1]
    w_down = w_out[0]
    contract_last = (((1,), (1,)), ((), ()))
    a = lax.dot_general(rows_x, w_gate, contract_last, preferred_element_type=jnp.float32)
    b = lax.dot_general(rows_x, w_up, contract_last, preferred_element_type=jnp.float32)
    sig = jax.nn.sigmoid(a)
    silu = a * sig
    hidden = (silu * b).astype(jnp.bfloat16)
    dh = lax.dot_general(rows_g, w_down, contract_last, preferred_element_type=jnp.float32)
    da = (dh * b * sig * (1.0 + a * (1.0 - sig))).astype(jnp.bfloat16)
    db = (dh * silu).astype(jnp.bfloat16)
    partial_rows = jnp.dot(da, w_gate, preferred_element_type=jnp.float32)
    partial_rows = partial_rows + jnp.dot(db, w_up, preferred_element_type=jnp.float32)
    summed = lax.psum_scatter(
        partial_rows.reshape(n_ep, cap, width).astype(jnp.bfloat16),
        "tp",
        scatter_dimension=2,
        tiled=True,
    )
    back = lax.all_to_all(summed, "ep", split_axis=0, concat_axis=0, tiled=True)
    picked = back.reshape(n_ep * cap, back.shape[2])[slot]
    in_grad = jnp.sum(
        picked.astype(jnp.float32).reshape(tok_dev, top, back.shape[2]), axis=1
    ).astype(jnp.bfloat16)
    contract_rows = (((0,), (0,)), ((), ()))
    own_in = jnp.stack(
        [
            lax.dot_general(da, rows_x, contract_rows, preferred_element_type=jnp.float32),
            lax.dot_general(db, rows_x, contract_rows, preferred_element_type=jnp.float32),
        ]
    ).astype(jnp.bfloat16)[None]
    own_out = lax.dot_general(
        hidden, rows_g, contract_rows, preferred_element_type=jnp.float32
    ).astype(jnp.bfloat16)[None]
    half_bit = n_ep.bit_length() - 2
    other_in, other_out = partner((own_in, own_out), "ep", half_bit)
    grad_in = (own_in.astype(jnp.float32) + other_in.astype(jnp.float32)).astype(jnp.bfloat16)
    grad_out = (own_out.astype(jnp.float32) + other_out.astype(jnp.float32)).astype(jnp.bfloat16)
    return (in_grad, grad_in, grad_out)


def solution(mesh):
    return jax.shard_map(
        body,
        mesh=mesh,
        in_specs=(
            P("ep", "tp"),
            P("ep", "tp"),
            P("ep", None),
            P("ep", None),
            P("ep", None, "tp", None),
            P("ep", "tp", None),
        ),
        out_specs=(P("ep", "tp"), P("ep", None, "tp", None), P("ep", "tp", None)),
        check_vma=False,
    )
```

profile of v0, /device:TPU:0, one launch (start us, length us, event | category | flops | bytes accessed | tf_op | source)
XLA Modules:
  0.0 534.7 jit_solution(16174911186118901653)
XLA Ops:
  7.2 0.7 all-gather.5.cloned.1.call-update
  7.9 0.8 copy.10
  8.7 0.1 eq.29
  8.8 0.1 eq.25
  8.9 1.2 reduce-window.6
  10.1 0.2 slice_reduce_fusion
  10.3 0.7 broadcast_multiply_fusion
  11.0 0.1 copy.9
  11.2 0.1 mul.53
  11.3 0.8 copy.13
  12.1 0.1 reshape.144
  12.2 0.1 fusion.20
  12.3 2.4 scatter_custom_fusion
  14.8 6.8 %gather_fusion = bf16[1024]{0:T(1024)(128)(2,1)S(1)} fusion(bf16[512]{0:T(512)(128)(2,1)S(1)} %reshape.144, s32[1024]{0:T(1024)S(1)} %get-tuple-element.7), kind=kCustom, calls=%fused_computation | custom fusion | bytes 8192 | tf_op jit(solution)/shard_map/gather | solution.py:38
  21.6 0.1 broadcast_in_dim.35
  21.7 13.9 %all-gather.5.cloned.1.call-done = bf16[128,4096]{1,0:T(8,128)(2,1)} async-done(((bf16[128,512]{1,0:T(8,128)(2,1)}), bf16[128,4096]{1,0:T(8,128)(2,1)}) %all-gather.5.cloned.1.call-update) | async-done | bytes 1048592 | tf_op jit(solution)/shard_map/all_gather | solution.py:40
  35.6 16.4 %gather_fusion.2 = bf16[1024,4096]{1,0:T(8,128)(2,1)} fusion(bf16[128,4096]{1,0:T(8,128)(2,1)} %all-gather.5.cloned.1.call-done, s32[1024]{0:T(1024)S(1)} %get-tuple-element.8), kind=kCustom, calls=%fused_computation.2 | custom fusion | bytes 16781312 | tf_op jit(solution)/shard_map/gather | solution.py:43
  52.0 7.2 %broadcast_select_fusion = bf16[16,64,4096]{2,1,0:T(8,128)(2,1)} fusion(bf16[16,64,4096]{2,1,0:T(8,128)(2,1)} %bitcast.56, pred[16,64]{1,0:T(8,128)(4,1)S(1)} %broadcast_in_dim.35), kind=kLoop, calls=%fused_computation.8 | loop fusion | flops 4194304 | bytes 16778240 | tf_op jit(solution)/shard_map/jit(_where)/select_n | solution.py:43
  59.2 7.0 %all-to-all-start.1 = ((bf16[16,64,4096]{2,1,0:T(8,128)(2,1)}), bf16[16,64,4096]{2,1,0:T(8,128)(2,1)}, u32[]{:S(2)}, u32[]{:S(2)}) async-start(bf16[16,64,4096]{2,1,0:T(8,128)(2,1)} %broadcast_select_fusion), calls=%async_computation.1 | async-start | bytes 16777216 | tf_op jit(solution)/shard_map/all_to_all | solution.py:49
  66.3 0.0 all-gather.3.cloned.1.call-start
  66.3 0.7 all-gather.3.cloned.1.call-update
  67.0 0.1 mul.55
  67.1 25.2 %all-gather.3.cloned.1.call-done = bf16[128,4096]{1,0:T(8,128)(2,1)} async-done(((bf16[128,512]{1,0:T(8,128)(2,1)}), bf16[128,4096]{1,0:T(8,128)(2,1)}) %all-gather.3.cloned.1.call-update) | async-done | bytes 1048592 | tf_op jit(solution)/shard_map/all_gather | solution.py:41
  92.3 16.4 %gather_fusion.1 = bf16[1024,4096]{1,0:T(8,128)(2,1)} fusion(bf16[128,4096]{1,0:T(8,128)(2,1)} %all-gather.3.cloned.1.call-done, s32[1024]{0:T(1024)S(1)} %get-tuple-element.8), kind=kCustom, calls=%fused_computation.1 | custom fusion | bytes 16781312 | tf_op jit(solution)/shard_map/gather | solution.py:44
  108.7 10.0 %fusion = bf16[16,64,4096]{2,1,0:T(8,128)(2,1)} fusion(bf16[16,64,4096]{2,1,0:T(8,128)(2,1)} %bitcast.57, f32[16,64]{1,0:T(8,128)S(1)} %mul.55), kind=kLoop, calls=%fused_computation.6 | loop fusion | flops 12582912 | bytes 16781312 | tf_op jit(solution)/shard_map/convert_element_type | solution.py:44
  118.7 93.8 %all-to-all-done.1 = bf16[16,64,4096]{2,1,0:T(8,128)(2,1)} async-done(((bf16[16,64,4096]{2,1,0:T(8,128)(2,1)}), bf16[16,64,4096]{2,1,0:T(8,128)(2,1)}, u32[]{:S(2)}, u32[]{:S(2)}) %all-to-all-start.1) | async-done | bytes 8388640 | tf_op jit(solution)/shard_map/all_to_all | solution.py:49
  212.5 11.8 %all-to-all-start = ((bf16[16,64,4096]{2,1,0:T(8,128)(2,1)}), bf16[16,64,4096]{2,1,0:T(8,128)(2,1)}, u32[]{:S(2)}, u32[]{:S(2)}) async-start(bf16[16,64,4096]{2,1,0:T(8,128)(2,1)} %fusion), calls=%async_computation | async-start | bytes 16777216 | tf_op jit(solution)/shard_map/all_to_all | solution.py:50
  224.3 0.2 reduce-scatter.2.cloned.1.call-start
  224.5 6.8 %fusion.6 = f32[1024,192]{0,1:T(8,128)S(1)} fusion(bf16[1024,4096]{1,0:T(8,128)(2,1)} %bitcast.7, bf16[1,2,192,4096]{3,2,1,0:T(8,128)(2,1)} %param.10), kind=kOutput, calls=%fused_computation.20 | convolution fusion | flops 1610612736 | bytes 10747904 | tf_op jit(solution)/shard_map/dot_general | solution.py:59
  231.4 7.2 %fusion.9 = f32[1024,192]{0,1:T(8,128)} fusion(bf16[1024,4096]{1,0:T(8,128)(2,1)} %bitcast.7, bf16[1,2,192,4096]{3,2,1,0:T(8,128)(2,1)S(1)} %copy-done.3), kind=kOutput, calls=%fused_computation.23 | convolution fusion | flops 1610612736 | bytes 10747904 | tf_op jit(solution)/shard_map/dot_general | solution.py:60
  238.5 119.4 %all-to-all-done = bf16[16,64,4096]{2,1,0:T(8,128)(2,1)} async-done(((bf16[16,64,4096]{2,1,0:T(8,128)(2,1)}), bf16[16,64,4096]{2,1,0:T(8,128)(2,1)}, u32[]{:S(2)}, u32[]{:S(2)}) %all-to-all-start) | async-done | bytes 8388640 | tf_op jit(solution)/shard_map/all_to_all | solution.py:50
  357.9 6.7 %multiply_convert_fusion.1 = (bf16[1024,192]{0,1:T(8,128)(2,1)S(1)}, bf16[1024,192]{0,1:T(8,128)(2,1)S(1)}) fusion(f32[1024,192]{0,1:T(8,128)S(1)} %fusion.6, f32[1024,192]{0,1:T(8,128)} %fusion.9, bf16[1024,4096]{1,0:T(8,128)(2,1)} %bitcast.4, bf16[1,192,4096]{2,1,0:T(8,128)(2,1)S(1)} %copy-done), kind=kOutput, calls=%fused_computation.32 | convolution fusion | flops 1613168640 | bytes 12320768 | tf_op jit(solution)/shard_map/dot_general | solution.py:64
  364.6 8.1 %fusion.4 = f32[1024,4096]{1,0:T(8,128)} fusion(bf16[1024,192]{0,1:T(8,128)(2,1)S(1)} %get-tuple-element.6, bf16[1,2,192,4096]{3,2,1,0:T(8,128)(2,1)S(1)} %copy-done.4), kind=kOutput, calls=%fused_computation.18 | convolution fusion | flops 1610612736 | bytes 18743296 | tf_op jit(solution)/shard_map/dot_general | solution.py:67
  372.8 11.4 %add_convert_fusion = bf16[1024,4096]{1,0:T(8,128)(2,1)} fusion(f32[1024,4096]{1,0:T(8,128)} %fusion.4, bf16[1024,192]{0,1:T(8,128)(2,1)S(1)} %get-tuple-element.5, bf16[1,2,192,4096]{3,2,1,0:T(8,128)(2,1)S(1)} %copy-done.4), kind=kOutput, calls=%fused_computation.7 | convolution fusion | flops 1619001344 | bytes 27131904 | tf_op jit(solution)/shard_map/dot_general | solution.py:68
  384.2 5.4 %fusion.1 = bf16[1,1,192,4096]{3,2,1,0:T(8,128)(2,1)S(1)} fusion(bf16[1024,192]{0,1:T(8,128)(2,1)S(1)} %get-tuple-element.6, bf16[1024,4096]{1,0:T(8,128)(2,1)} %bitcast.7), kind=kOutput, calls=%fused_computation.13 | convolution fusion | flops 1611399168 | bytes 10354688 | tf_op jit(solution)/shard_map/dot_general | solution.py:83
  389.7 5.8 %fusion.2 = bf16[1,1,192,4096]{3,2,1,0:T(8,128)(2,1)S(1)} fusion(bf16[1024,192]{0,1:T(8,128)(2,1)S(1)} %get-tuple-element.5, bf16[1024,4096]{1,0:T(8,128)(2,1)} %bitcast.7), kind=kOutput, calls=%fused_computation.14 | convolution fusion | flops 1611399168 | bytes 10354688 | tf_op jit(solution)/shard_map/dot_general | solution.py:84
  395.4 1.9 pad_maximum_fusion
  397.4 0.2 copy-done.2
  397.6 5.3 fusion.3
  402.9 3.7 collective-permute-start.1
  406.6 92.6 %collective-permute-done.1 = bf16[1,192,4096]{2,1,0:T(8,128)(2,1)S(1)} collective-permute-done((bf16[1,192,4096]{2,1,0:T(8,128)(2,1)S(1)}, bf16[1,192,4096]{2,1,0:T(8,128)(2,1)S(1)}, u32[]{:S(2)}, u32[]{:S(2)}) %collective-permute-start.1) | collective-permute-done | bytes 1572896 | tf_op jit(solution)/shard_map/ppermute | solution.py:14
  499.2 1.7 add_convert_fusion.2
  500.9 9.9 %all-to-all-start.2 = ((bf16[16,64,512]{2,1,0:T(8,128)(2,1)}), bf16[16,64,512]{2,1,0:T(8,128)(2,1)S(1)}, u32[]{:S(2)}, u32[]{:S(2)}) async-start(bf16[16,64,512]{2,1,0:T(8,128)(2,1)} %reduce-scatter.2.cloned.1.call-done), calls=%async_computation.3 | async-start | bytes 2097152 | tf_op jit(solution)/shard_map/all_to_all | solution.py:75
  510.8 5.8 %add_convert_fusion.1 = bf16[1,2,192,4096]{3,2,1,0:T(8,128)(2,1)} fusion(bf16[1,2,192,4096]{3,2,1,0:T(8,128)(2,1)} %collective-permute-done, bf16[1,1,192,4096]{3,2,1,0:T(8,128)(2,1)} %copy-done.2, bf16[1,1,192,4096]{3,2,1,0:T(8,128)(2,1)} %copy-done.1), kind=kLoop, calls=%fused_computation.9 | loop fusion | flops 7864320 | bytes 9437184 | tf_op jit(solution)/shard_map/convert_element_type | solution.py:92
  516.6 8.2 %all-to-all-done.2 = bf16[16,64,512]{2,1,0:T(8,128)(2,1)S(1)} async-done(((bf16[16,64,512]{2,1,0:T(8,128)(2,1)}), bf16[16,64,512]{2,1,0:T(8,128)(2,1)S(1)}, u32[]{:S(2)}, u32[]{:S(2)}) %all-to-all-start.2) | async-done | bytes 1048608 | tf_op jit(solution)/shard_map/all_to_all | solution.py:75
  524.7 2.0 gather_fusion.3
  526.7 0.1 gather.21
  526.8 1.3 reduce_sum.25
  (24 shorter events, 0.2 us)
Async XLA Ops:
  7.2 350.7 %copy-start = (bf16[1,192,4096]{2,1,0:T(8,128)(2,1)S(1)}, bf16[1,192,4096]{2,1,0:T(8,128)(2,1)}, u32[]{:S(2)}) copy-start(bf16[1,192,4096]{2,1,0:T(8,128)(2,1)} %param.11) | copy-start | bytes 4718596
  7.2 28.4 %all-gather.5.cloned.1.call-start = ((), (), s32[]{:S(2)}) async-start(), calls=%async_computation.5 | async-start | bytes 1179648 | tf_op jit(solution)/shard_map/all_gather | solution.py:40
  59.2 153.3 %all-to-all-start.1 = ((bf16[16,64,4096]{2,1,0:T(8,128)(2,1)}), bf16[16,64,4096]{2,1,0:T(8,128)(2,1)}, u32[]{:S(2)}, u32[]{:S(2)}) async-start(bf16[16,64,4096]{2,1,0:T(8,128)(2,1)} %broadcast_select_fusion), calls=%async_computation.1 | async-start | bytes 16777216 | tf_op jit(solution)/shard_map/all_to_all | solution.py:49
  66.3 26.0 %all-gather.3.cloned.1.call-start = ((), (), s32[]{:S(2)}) async-start(), calls=%async_computation.4 | async-start | bytes 1179648 | tf_op jit(solution)/shard_map/all_gather | solution.py:41
  212.5 145.4 %all-to-all-start = ((bf16[16,64,4096]{2,1,0:T(8,128)(2,1)}), bf16[16,64,4096]{2,1,0:T(8,128)(2,1)}, u32[]{:S(2)}, u32[]{:S(2)}) async-start(bf16[16,64,4096]{2,1,0:T(8,128)(2,1)} %fusion), calls=%async_computation | async-start | bytes 16777216 | tf_op jit(solution)/shard_map/all_to_all | solution.py:50
  224.3 276.6 %reduce-scatter.2.cloned.1.call-start = ((), (), s32[]{:S(2)}) async-start(), calls=%async_computation.6 | async-start | bytes 9437184 | tf_op jit(solution)/shard_map/reduce_scatter | solution.py:69
  224.5 6.9 %copy-start.3 = (bf16[1,2,192,4096]{3,2,1,0:T(8,128)(2,1)S(1)}, bf16[1,2,192,4096]{3,2,1,0:T(8,128)(2,1)}, u32[]{:S(2)}) copy-start(bf16[1,2,192,4096]{3,2,1,0:T(8,128)(2,1)} %param.10) | copy-start | bytes 9437188
  357.9 6.7 %copy-start.4 = (bf16[1,2,192,4096]{3,2,1,0:T(8,128)(2,1)S(1)}, bf16[1,2,192,4096]{3,2,1,0:T(8,128)(2,1)}, u32[]{:S(2)}) copy-start(bf16[1,2,192,4096]{3,2,1,0:T(8,128)(2,1)} %param.10) | copy-start | bytes 9437188
  389.6 5.8 %copy-start.1 = (bf16[1,1,192,4096]{3,2,1,0:T(8,128)(2,1)}, bf16[1,1,192,4096]{3,2,1,0:T(8,128)(2,1)S(1)}, u32[]{:S(2)}) copy-start(bf16[1,1,192,4096]{3,2,1,0:T(8,128)(2,1)S(1)} %fusion.1) | copy-start | bytes 4718596
  395.4 2.2 copy-start.2
  395.4 2.2 copy-start.5
  397.6 113.2 %collective-permute-start = (bf16[1,2,192,4096]{3,2,1,0:T(8,128)(2,1)}, bf16[1,2,192,4096]{3,2,1,0:T(8,128)(2,1)}, u32[]{:S(2)}, u32[]{:S(2)}) collective-permute-start(bf16[1,2,192,4096]{3,2,1,0:T(8,128)(2,1)} %pad_maximum_fusion), channel_id=1, source_target_pairs={{0,64},{64,0},{8,72},{72,8},{16,80},{80,16},{24,88},{88,24},{32,96... | collective-permute-start | bytes 9437192 | tf_op jit(solution)/shard_map/ppermute | solution.py:14
  402.9 96.3 %collective-permute-start.1 = (bf16[1,192,4096]{2,1,0:T(8,128)(2,1)S(1)}, bf16[1,192,4096]{2,1,0:T(8,128)(2,1)S(1)}, u32[]{:S(2)}, u32[]{:S(2)}) collective-permute-start(bf16[1,192,4096]{2,1,0:T(8,128)(2,1)S(1)} %fusion.3), channel_id=1, source_target_pairs={{0,64},{64,0},{8,72},{72,8},{16,80},{80,16},{24,88},{88,24},{32,96... | collective-permute-start | bytes 4718600 | tf_op jit(solution)/shard_map/ppermute | solution.py:14
  500.9 23.9 %all-to-all-start.2 = ((bf16[16,64,512]{2,1,0:T(8,128)(2,1)}), bf16[16,64,512]{2,1,0:T(8,128)(2,1)S(1)}, u32[]{:S(2)}, u32[]{:S(2)}) async-start(bf16[16,64,512]{2,1,0:T(8,128)(2,1)} %reduce-scatter.2.cloned.1.call-done), calls=%async_computation.3 | async-start | bytes 2097152 | tf_op jit(solution)/shard_map/all_to_all | solution.py:75
Sparse Core Ops, SparseCore 0:
  9.7 25.8 all-gather.4
  68.8 23.4 all-gather.2
  384.3 54.3 reduce-scatter.1
where the time goes:
time: 535 us
  waiting for transfers between devices  354 us (66%)
  matrix products  56.7 us (11%)
  local copies, waits for them, and re-layouts  47 us (9%)
  starting transfers between devices  32.6 us (6%)
  other arithmetic  30 us (6%)
  between operations  14 us (3%)
    all_to_all x1, waiting for transfers between devices, body(): lax.all_to_all(send_g, 'ep', split_axis=0, concat_axis=0, tiled=True)  119 us
    all_to_all x1, waiting for transfers between devices, body(): lax.all_to_all(send_x, 'ep', split_axis=0, concat_axis=0, tiled=True)  93.8 us
    ppermute x2, waiting for transfers between devices, partner(): return lax.ppermute(block, axis, route)  92.6 us
    all_gather x1, waiting for transfers between devices, body(): lax.all_gather(out_grad, 'tp', axis=1, tiled=True)  25.2 us
    gather x1, local copies, waits for them, and re-layouts, body(): full_g[tok_index].astype(jnp.float32)  16.4 us
    gather x1, local copies, waits for them, and re-layouts, body(): full_x[tok_index]  16.4 us
    all_gather x1, waiting for transfers between devices, body(): lax.all_gather(tokens, 'tp', axis=1, tiled=True)  13.9 us
    all_to_all x1, starting transfers between devices, body(): lax.all_to_all(send_g, 'ep', split_axis=0, concat_axis=0, tiled=True)  11.8 us
  transfers between devices with their start and end apart: 8, of which 6 were waited for; matrix products, arithmetic and copies ran while one was open for 15% of the time, Pallas kernels for 0%

commit v1 on v0

--- a/solution.py
+++ b/solution.py
@@ -2,6 +2,11 @@
 import jax.numpy as jnp
 from jax import lax
 from jax.sharding import PartitionSpec as P
+
+
+def gather_by_exchange(x, axis, dim):
+    copies = jnp.concatenate([x] * lax.axis_size(axis), axis=dim)
+    return lax.all_to_all(copies, axis, dim, dim, tiled=True)
 
 
 def partner(block, axis, apart):
@@ -37,7 +42,7 @@
     tok_index = local // top
     scale = jnp.where(valid, probs.reshape(-1)[local].astype(jnp.float32), 0.0)[:, None]
     full_x, full_g = (
-        lax.all_gather(tokens, "tp", axis=1, tiled=True),
+        gather_by_exchange(tokens, "tp", 1),
         lax.all_gather(out_grad, "tp", axis=1, tiled=True),
     )
     packed_x = jnp.where(valid[:, None], full_x[tok_index], jnp.zeros((), jnp.bfloat16))

time: 535 us -> 518 us (0.968)
  the two profiles are of different devices: /device:TPU:0 before, /device:TPU:16 now
where the time goes in v1:
time: 518 us
  waiting for transfers between devices  341 us (66%)
  matrix products  56.8 us (11%)
  local copies, waits for them, and re-layouts  42 us (8%)
  starting transfers between devices  33.9 us (7%)
  other arithmetic  29.3 us (6%)
  between operations  14.4 us (3%)
    all_to_all x1, waiting for transfers between devices, body(): lax.all_to_all(send_g, 'ep', split_axis=0, concat_axis=0, tiled=True)  119 us
    all_to_all x1, waiting for transfers between devices, body(): lax.all_to_all(send_x, 'ep', split_axis=0, concat_axis=0, tiled=True)  94 us
    ppermute x2, waiting for transfers between devices, partner(): return lax.ppermute(block, axis, route)  92.2 us
    all_gather x1, waiting for transfers between devices, body(): lax.all_gather(out_grad, 'tp', axis=1, tiled=True)  26 us
    gather x1, local copies, waits for them, and re-layouts, body(): full_g[tok_index].astype(jnp.float32)  16.4 us
    dot_general x1, matrix products, body(): jnp.dot(db, w_up, preferred_element_type=jnp.float32)  11.4 us
  transfers between devices with their start and end apart: 8, of which 6 were waited for; matrix products, arithmetic and copies ran while one was open for 15% of the time, Pallas kernels for 0%

profile of v1, /device:TPU:16, one launch (start us, length us, event | category | flops | bytes accessed | tf_op | source)
XLA Modules:
  0.0 517.6 jit_solution(3885076570865866522)
XLA Ops:
  7.2 1.1 copy.25
  8.6 1.3 copy.33
  9.9 4.8 all-to-all-start.1
  14.7 0.1 copy.21
  14.8 0.1 eq.29
  14.9 0.1 eq.25
  15.0 1.2 reduce-window.6
  16.2 0.2 slice_reduce_fusion
  16.4 0.1 copy.20
  16.6 0.1 mul.53
  16.7 0.1 copy.24
  16.8 0.1 reshape.146
  16.9 0.1 fusion.20
  17.1 2.4 scatter_custom_fusion
  19.5 6.8 %gather_fusion = bf16[1024]{0:T(1024)(128)(2,1)S(1)} fusion(bf16[512]{0:T(512)(128)(2,1)S(1)} %reshape.146, s32[1024]{0:T(1024)S(1)} %get-tuple-element.7), kind=kCustom, calls=%fused_computation | custom fusion | bytes 8192 | tf_op jit(solution)/shard_map/gather | solution.py:43
  26.4 1.1 all-to-all-done.1
  27.5 1.0 copy-done.3
  28.5 1.3 copy.36
  29.8 7.8 %gather_fusion.2 = bf16[1024,4096]{1,0:T(8,128)(2,1)} fusion(bf16[128,4096]{1,0:T(8,128)(2,1)S(1)} %bitcast.58, s32[1024]{0:T(1024)S(1)} %get-tuple-element.8), kind=kCustom, calls=%fused_computation.2 | custom fusion | bytes 16781312 | tf_op jit(solution)/shard_map/gather | solution.py:48
  37.6 7.2 %broadcast_select_fusion = bf16[16,64,4096]{2,1,0:T(8,128)(2,1)} fusion(bf16[16,64,4096]{2,1,0:T(8,128)(2,1)} %bitcast.60, pred[16,64]{1,0:T(8,128)(4,1)S(1)} %broadcast_in_dim.35), kind=kLoop, calls=%fused_computation.8 | loop fusion | flops 4194304 | bytes 16778240 | tf_op jit(solution)/shard_map/jit(_where)/select_n | solution.py:48
  44.8 7.9 %all-to-all-start.2 = ((bf16[16,64,4096]{2,1,0:T(8,128)(2,1)}), bf16[16,64,4096]{2,1,0:T(8,128)(2,1)}, u32[]{:S(2)}, u32[]{:S(2)}) async-start(bf16[16,64,4096]{2,1,0:T(8,128)(2,1)} %broadcast_select_fusion), calls=%async_computation.2 | async-start | bytes 16777216 | tf_op jit(solution)/shard_map/all_to_all | solution.py:54
  52.8 0.7 all-gather.2.cloned.1.call-update
  53.6 26.0 %all-gather.2.cloned.1.call-done = bf16[128,4096]{1,0:T(8,128)(2,1)} async-done(((bf16[128,512]{1,0:T(8,128)(2,1)}), bf16[128,4096]{1,0:T(8,128)(2,1)}) %all-gather.2.cloned.1.call-update) | async-done | bytes 1048592 | tf_op jit(solution)/shard_map/all_gather | solution.py:46
  79.5 16.4 %gather_fusion.1 = bf16[1024,4096]{1,0:T(8,128)(2,1)} fusion(bf16[128,4096]{1,0:T(8,128)(2,1)} %all-gather.2.cloned.1.call-done, s32[1024]{0:T(1024)S(1)} %get-tuple-element.8), kind=kCustom, calls=%fused_computation.1 | custom fusion | bytes 16781312 | tf_op jit(solution)/shard_map/gather | solution.py:49
  96.0 10.0 %fusion = bf16[16,64,4096]{2,1,0:T(8,128)(2,1)} fusion(bf16[16,64,4096]{2,1,0:T(8,128)(2,1)} %bitcast.61, f32[16,64]{1,0:T(8,128)S(1)} %mul.55), kind=kLoop, calls=%fused_computation.6 | loop fusion | flops 12582912 | bytes 16781312 | tf_op jit(solution)/shard_map/convert_element_type | solution.py:49
  106.0 94.0 %all-to-all-done.2 = bf16[16,64,4096]{2,1,0:T(8,128)(2,1)} async-done(((bf16[16,64,4096]{2,1,0:T(8,128)(2,1)}), bf16[16,64,4096]{2,1,0:T(8,128)(2,1)}, u32[]{:S(2)}, u32[]{:S(2)}) %all-to-all-start.2) | async-done | bytes 8388640 | tf_op jit(solution)/shard_map/all_to_all | solution.py:54
  200.0 8.4 %all-to-all-start = ((bf16[16,64,4096]{2,1,0:T(8,128)(2,1)}), bf16[16,64,4096]{2,1,0:T(8,128)(2,1)}, u32[]{:S(2)}, u32[]{:S(2)}) async-start(bf16[16,64,4096]{2,1,0:T(8,128)(2,1)} %fusion), calls=%async_computation | async-start | bytes 16777216 | tf_op jit(solution)/shard_map/all_to_all | solution.py:55
  208.4 0.2 reduce-scatter.2.cloned.1.call-start
  208.6 6.8 %fusion.6 = f32[1024,192]{0,1:T(8,128)S(1)} fusion(bf16[1024,4096]{1,0:T(8,128)(2,1)} %bitcast.8, bf16[1,2,192,4096]{3,2,1,0:T(8,128)(2,1)} %param.10), kind=kOutput, calls=%fused_computation.20 | convolution fusion | flops 1610612736 | bytes 10747904 | tf_op jit(solution)/shard_map/dot_general | solution.py:64
  215.5 7.2 %fusion.9 = f32[1024,192]{0,1:T(8,128)} fusion(bf16[1024,4096]{1,0:T(8,128)(2,1)} %bitcast.8, bf16[1,2,192,4096]{3,2,1,0:T(8,128)(2,1)S(1)} %copy-done.4), kind=kOutput, calls=%fused_computation.23 | convolution fusion | flops 1610612736 | bytes 10747904 | tf_op jit(solution)/shard_map/dot_general | solution.py:65
  222.6 119.4 %all-to-all-done = bf16[16,64,4096]{2,1,0:T(8,128)(2,1)} async-done(((bf16[16,64,4096]{2,1,0:T(8,128)(2,1)}), bf16[16,64,4096]{2,1,0:T(8,128)(2,1)}, u32[]{:S(2)}, u32[]{:S(2)}) %all-to-all-start) | async-done | bytes 8388640 | tf_op jit(solution)/shard_map/all_to_all | solution.py:55
  342.1 6.7 %multiply_convert_fusion.1 = (bf16[1024,192]{0,1:T(8,128)(2,1)S(1)}, bf16[1024,192]{0,1:T(8,128)(2,1)S(1)}) fusion(f32[1024,192]{0,1:T(8,128)S(1)} %fusion.6, f32[1024,192]{0,1:T(8,128)} %fusion.9, bf16[1024,4096]{1,0:T(8,128)(2,1)} %bitcast.4, bf16[1,192,4096]{2,1,0:T(8,128)(2,1)S(1)} %copy-done), kind=kOutput, calls=%fused_computation.32 | convolution fusion | flops 1613168640 | bytes 12320768 | tf_op jit(solution)/shard_map/dot_general | solution.py:69
  348.8 8.1 %fusion.4 = f32[1024,4096]{1,0:T(8,128)} fusion(bf16[1024,192]{0,1:T(8,128)(2,1)S(1)} %get-tuple-element.6, bf16[1,2,192,4096]{3,2,1,0:T(8,128)(2,1)S(1)} %copy-done.5), kind=kOutput, calls=%fused_computation.18 | convolution fusion | flops 1610612736 | bytes 18743296 | tf_op jit(solution)/shard_map/dot_general | solution.py:72
  357.0 11.4 %add_convert_fusion = bf16[1024,4096]{1,0:T(8,128)(2,1)} fusion(f32[1024,4096]{1,0:T(8,128)} %fusion.4, bf16[1024,192]{0,1:T(8,128)(2,1)S(1)} %get-tuple-element.5, bf16[1,2,192,4096]{3,2,1,0:T(8,128)(2,1)S(1)} %copy-done.5), kind=kOutput, calls=%fused_computation.7 | convolution fusion | flops 1619001344 | bytes 27131904 | tf_op jit(solution)/shard_map/dot_general | solution.py:73
  368.4 5.4 %fusion.1 = bf16[1,1,192,4096]{3,2,1,0:T(8,128)(2,1)S(1)} fusion(bf16[1024,192]{0,1:T(8,128)(2,1)S(1)} %get-tuple-element.6, bf16[1024,4096]{1,0:T(8,128)(2,1)} %bitcast.8), kind=kOutput, calls=%fused_computation.13 | convolution fusion | flops 1611399168 | bytes 10354688 | tf_op jit(solution)/shard_map/dot_general | solution.py:88
  373.8 5.8 %fusion.2 = bf16[1,1,192,4096]{3,2,1,0:T(8,128)(2,1)S(1)} fusion(bf16[1024,192]{0,1:T(8,128)(2,1)S(1)} %get-tuple-element.5, bf16[1024,4096]{1,0:T(8,128)(2,1)} %bitcast.8), kind=kOutput, calls=%fused_computation.14 | convolution fusion | flops 1611399168 | bytes 10354688 | tf_op jit(solution)/shard_map/dot_general | solution.py:89
  379.6 2.0 pad_maximum_fusion
  381.6 0.4 copy-done.2
  382.0 5.3 %fusion.3 = bf16[1,192,4096]{2,1,0:T(8,128)(2,1)S(1)} fusion(bf16[1024,4096]{1,0:T(8,128)(2,1)} %bitcast.4, f32[1024,192]{0,1:T(8,128)S(1)} %copy-done.8, f32[1024,192]{0,1:T(8,128)S(1)} %fusion.6), kind=kOutput, calls=%fused_computation.15 | convolution fusion | flops 1612578816 | bytes 11534336 | tf_op jit(solution)/shard_map/dot_general | solution.py:92
  387.3 3.6 collective-permute-start.1
  391.0 92.2 %collective-permute-done.1 = bf16[1,192,4096]{2,1,0:T(8,128)(2,1)S(1)} collective-permute-done((bf16[1,192,4096]{2,1,0:T(8,128)(2,1)S(1)}, bf16[1,192,4096]{2,1,0:T(8,128)(2,1)S(1)}, u32[]{:S(2)}, u32[]{:S(2)}) %collective-permute-start.1) | collective-permute-done | bytes 1572896 | tf_op jit(solution)/shard_map/ppermute | solution.py:19
  483.2 1.7 add_convert_fusion.2
  484.9 8.8 %all-to-all-start.3 = ((bf16[16,64,512]{2,1,0:T(8,128)(2,1)}), bf16[16,64,512]{2,1,0:T(8,128)(2,1)S(1)}, u32[]{:S(2)}, u32[]{:S(2)}) async-start(bf16[16,64,512]{2,1,0:T(8,128)(2,1)} %reduce-scatter.2.cloned.1.call-done), calls=%async_computation.4 | async-start | bytes 2097152 | tf_op jit(solution)/shard_map/all_to_all | solution.py:80
  493.7 5.8 %add_convert_fusion.1 = bf16[1,2,192,4096]{3,2,1,0:T(8,128)(2,1)} fusion(bf16[1,2,192,4096]{3,2,1,0:T(8,128)(2,1)} %collective-permute-done, bf16[1,1,192,4096]{3,2,1,0:T(8,128)(2,1)} %copy-done.2, bf16[1,1,192,4096]{3,2,1,0:T(8,128)(2,1)} %copy-done.1), kind=kLoop, calls=%fused_computation.9 | loop fusion | flops 7864320 | bytes 9437184 | tf_op jit(solution)/shard_map/convert_element_type | solution.py:97
  499.5 7.9 %all-to-all-done.3 = bf16[16,64,512]{2,1,0:T(8,128)(2,1)S(1)} async-done(((bf16[16,64,512]{2,1,0:T(8,128)(2,1)}), bf16[16,64,512]{2,1,0:T(8,128)(2,1)S(1)}, u32[]{:S(2)}, u32[]{:S(2)}) %all-to-all-start.3) | async-done | bytes 1048608 | tf_op jit(solution)/shard_map/all_to_all | solution.py:80
  507.4 2.0 gather_fusion.3
  509.3 0.1 gather.21
  509.5 1.3 reduce_sum.25
  (40 shorter events, 0.5 us)
Async XLA Ops:
  7.2 334.9 %copy-start = (bf16[1,192,4096]{2,1,0:T(8,128)(2,1)S(1)}, bf16[1,192,4096]{2,1,0:T(8,128)(2,1)}, u32[]{:S(2)}) copy-start(bf16[1,192,4096]{2,1,0:T(8,128)(2,1)} %param.11) | copy-start | bytes 4718596
  8.3 6.4 %copy-start.6 = (s32[128,4]{0,1:T(4,128)S(1)}, s32[128,4]{0,1:T(4,128)}, u32[]{:S(2)}) copy-start(s32[128,4]{0,1:T(4,128)} %param.8) | copy-start | bytes 6148
  8.4 8.3 %copy-start.7 = (bf16[128,4]{0,1:T(4,128)(2,1)S(1)}, bf16[128,4]{0,1:T(4,128)(2,1)}, u32[]{:S(2)}) copy-start(bf16[128,4]{0,1:T(4,128)(2,1)} %param.9) | copy-start | bytes 3076
  9.9 17.6 %all-to-all-start.1 = ((bf16[128,8,512]{2,0,1:T(8,128)(2,1)}), bf16[128,8,512]{2,0,1:T(8,128)(2,1)S(1)}, u32[]{:S(2)}, u32[]{:S(2)}) async-start(bf16[128,8,512]{2,0,1:T(8,128)(2,1)} %copy.33), calls=%async_computation.1 | async-start | bytes 2097152 | tf_op jit(solution)/shard_map/all_to_all | solution.py:9
  27.5 1.0 copy-start.3
  44.8 155.2 %all-to-all-start.2 = ((bf16[16,64,4096]{2,1,0:T(8,128)(2,1)}), bf16[16,64,4096]{2,1,0:T(8,128)(2,1)}, u32[]{:S(2)}, u32[]{:S(2)}) async-start(bf16[16,64,4096]{2,1,0:T(8,128)(2,1)} %broadcast_select_fusion), calls=%async_computation.2 | async-start | bytes 16777216 | tf_op jit(solution)/shard_map/all_to_all | solution.py:54
  52.7 26.8 %all-gather.2.cloned.1.call-start = ((), (), s32[]{:S(2)}) async-start(), calls=%async_computation.5 | async-start | bytes 1179648 | tf_op jit(solution)/shard_map/all_gather | solution.py:46
  200.0 142.1 %all-to-all-start = ((bf16[16,64,4096]{2,1,0:T(8,128)(2,1)}), bf16[16,64,4096]{2,1,0:T(8,128)(2,1)}, u32[]{:S(2)}, u32[]{:S(2)}) async-start(bf16[16,64,4096]{2,1,0:T(8,128)(2,1)} %fusion), calls=%async_computation | async-start | bytes 16777216 | tf_op jit(solution)/shard_map/all_to_all | solution.py:55
  208.4 276.5 %reduce-scatter.2.cloned.1.call-start = ((), (), s32[]{:S(2)}) async-start(), calls=%async_computation.6 | async-start | bytes 9437184 | tf_op jit(solution)/shard_map/reduce_scatter | solution.py:74
  208.6 6.9 %copy-start.4 = (bf16[1,2,192,4096]{3,2,1,0:T(8,128)(2,1)S(1)}, bf16[1,2,192,4096]{3,2,1,0:T(8,128)(2,1)}, u32[]{:S(2)}) copy-start(bf16[1,2,192,4096]{3,2,1,0:T(8,128)(2,1)} %param.10) | copy-start | bytes 9437188
  342.1 6.7 %copy-start.5 = (bf16[1,2,192,4096]{3,2,1,0:T(8,128)(2,1)S(1)}, bf16[1,2,192,4096]{3,2,1,0:T(8,128)(2,1)}, u32[]{:S(2)}) copy-start(bf16[1,2,192,4096]{3,2,1,0:T(8,128)(2,1)} %param.10) | copy-start | bytes 9437188
  373.8 5.8 %copy-start.1 = (bf16[1,1,192,4096]{3,2,1,0:T(8,128)(2,1)}, bf16[1,1,192,4096]{3,2,1,0:T(8,128)(2,1)S(1)}, u32[]{:S(2)}) copy-start(bf16[1,1,192,4096]{3,2,1,0:T(8,128)(2,1)S(1)} %fusion.1) | copy-start | bytes 4718596
  379.6 2.4 copy-start.2
  379.6 2.4 copy-start.8
  382.0 111.7 %collective-permute-start = (bf16[1,2,192,4096]{3,2,1,0:T(8,128)(2,1)}, bf16[1,2,192,4096]{3,2,1,0:T(8,128)(2,1)}, u32[]{:S(2)}, u32[]{:S(2)}) collective-permute-start(bf16[1,2,192,4096]{3,2,1,0:T(8,128)(2,1)} %pad_maximum_fusion), channel_id=1, source_target_pairs={{0,64},{64,0},{8,72},{72,8},{16,80},{80,16},{24,88},{88,24},{32,96... | collective-permute-start | bytes 9437192 | tf_op jit(solution)/shard_map/ppermute | solution.py:19
  387.3 95.8 %collective-permute-start.1 = (bf16[1,192,4096]{2,1,0:T(8,128)(2,1)S(1)}, bf16[1,192,4096]{2,1,0:T(8,128)(2,1)S(1)}, u32[]{:S(2)}, u32[]{:S(2)}) collective-permute-start(bf16[1,192,4096]{2,1,0:T(8,128)(2,1)S(1)} %fusion.3), channel_id=1, source_target_pairs={{0,64},{64,0},{8,72},{72,8},{16,80},{80,16},{24,88},{88,24},{32,96... | collective-permute-start | bytes 4718600 | tf_op jit(solution)/shard_map/ppermute | solution.py:19
  484.9 22.5 %all-to-all-start.3 = ((bf16[16,64,512]{2,1,0:T(8,128)(2,1)}), bf16[16,64,512]{2,1,0:T(8,128)(2,1)S(1)}, u32[]{:S(2)}, u32[]{:S(2)}) async-start(bf16[16,64,512]{2,1,0:T(8,128)(2,1)} %reduce-scatter.2.cloned.1.call-done), calls=%async_computation.4 | async-start | bytes 2097152 | tf_op jit(solution)/shard_map/all_to_all | solution.py:80
Sparse Core Ops, SparseCore 0:
  55.3 24.2 all-gather.1
  368.5 53.7 reduce-scatter.1
